TPU v7x, 32 devices: a whole 2x2x4 slice. The times are simulated.
32 devices in a mesh: batch: 8 (over y, x, core), slab: 4 (over z).
Axes of the slice: x: 2, y: 2, z: 4, core: 2. Of those that a mesh axis runs over, the one named last changes fastest.
Arguments:
- points: bfloat16 [7, 35, 16384], P(None, None, ('batch', 'slab')), may hold values from -6 to 6
- point_counts: int32 [16384], P(('batch', 'slab')), may hold values from 1 to 35, as said below
- voxel_cells: int32 [16384], P(('batch', 'slab')), may hold values from 0 to 4095, as said below
- pos_anchors: int32 [8, 40], P('batch'), may hold values from 0 to 1023, as said below
- pos_counts: int32 [8], P('batch'), may hold values from 0 to 40, as said below
- reg_targets: float32 [8, 14, 16, 32], P('batch'), may hold values from -6 to 6
- params: float32 [2537584], P('slab')
- moment1: float32 [2537584], P('slab'), may hold values from -1.9073486e-06 to 1.9073486e-06
- moment2: float32 [2537584], P('slab'), may hold values from 1.5763025e-15 to 6.30521e-15
Outputs:
- head_maps: float32 [8, 16, 16, 32], P('batch', None, 'slab')
- points_grad: float32 [7, 35, 16384], P(None, None, ('batch', 'slab'))
- new_moment1: float32 [2537584], P('slab')
- new_moment2: float32 [2537584], P('slab')
- new_params: float32 [2537584], P('slab')
- grad_norm: float32 [], replicated
Inputs may be any that keep to these rules, and one draw needn't show every extreme that they name: `point_counts`: at least one point; every block of 512 voxels has a voxel with 35. `voxel_cells`: distinct within each block of 512 voxels (one scene, one slab). `pos_anchors`: distinct within a scene. `pos_counts`: some scene has 40, some has none.
All inputs are finite; a program needn't handle non-finite values.
Results may differ from a plain program's by a relative error of at most 0.017.
Values may be sent and summed in bfloat16 or wider, within the bound.
No kernel may reach another device: no remote copies, remote signals or barrier semaphores. Data moves between devices by JAX's collectives and lax.ppermute only.
A program may use at most 192 MiB of HBM per device.

v0:
```python
import math

import jax
import jax.numpy as jnp
from jax import lax
from jax.sharding import PartitionSpec as P

VF1 = 16
VF2 = 64
FC = 128
C3 = 64
R1 = 128
R3 = 256
UP = 256
STEP = 10
GY = 32
GX = 64


highest = lax.Precision.HIGHEST
beta_one = 0.9
beta_two = 0.999
adam_eps = 1e-08
learn_rate = 0.02
weight_decay = 0.01
clip_level = 0.002


def extended(x, sides, width):
    for axis, dim in sides:
        size, length = (lax.axis_size(axis), x.shape[dim])
        up = [(i, (i + 1) % size) for i in range(size - 1)]
        down = [(j, i) for i, j in up]
        last = lax.slice_in_dim(x, length - width, length, axis=dim)
        initial = lax.slice_in_dim(x, 0, width, axis=dim)
        before = lax.ppermute(last, axis, up)
        after = lax.ppermute(initial, axis, down)
        x = jnp.concatenate([before, x, after], axis=dim)
    return x


def from_behind(value, axis, steps):
    count = lax.axis_size(axis)
    initial, last = (max(0, -steps), min(count, count - steps))
    return lax.ppermute(value, axis, [(source, source + steps) for source in range(initial, last)])


def round_low(values):
    return lax.optimization_barrier(values.astype(jnp.bfloat16)).astype(jnp.float32)


def rounded(values):
    return lax.optimization_barrier(values.astype(jnp.bfloat16)).astype(jnp.float32)


def layer_shapes():
    return [
        (VF1, 7),
        (VF2, 2 * VF1),
        (FC, 2 * VF2),
        (3, 3, 3, FC, C3),
        (3, 3, 3, C3, C3),
        (3, 3, 3, C3, C3),
        (3, 3, 2 * C3, R1),
        (3, 3, R1, R1),
        (3, 3, R1, R3),
        (3, 3, R1, UP),
        (2, 2, R1, UP),
        (4, 4, R3, UP),
        (3 * UP, 16),
    ]


def unpack(flat_values):
    pieces = []
    offset = 0
    for layer_shape in layer_shapes():
        entries = math.prod(layer_shape)
        pieces.append(flat_values[offset : offset + entries].reshape(layer_shape))
        offset += entries
    return pieces


def vfe_forward(vfe_one, vfe_two, vfe_three, cloud_points, counts):
    slots = jnp.arange(cloud_points.shape[1], dtype=jnp.int32)
    valid = (slots[:, None] < counts[None, :]).astype(jnp.float32)
    inverse = 1.0 / counts.astype(jnp.float32)
    first_part = jax.nn.silu(jnp.einsum("oc,cpv->opv", vfe_one, cloud_points, precision=highest))
    first_mean = jnp.sum(first_part * valid, axis=1) * inverse
    joined_one = rounded(
        jnp.concatenate([first_part, jnp.broadcast_to(first_mean[:, None, :], first_part.shape)], 0)
    )
    second_part = jax.nn.silu(jnp.einsum("oc,cpv->opv", vfe_two, joined_one, precision=highest))
    second_mean = jnp.sum(second_part * valid, axis=1) * inverse
    joined_two = rounded(
        jnp.concatenate(
            [second_part, jnp.broadcast_to(second_mean[:, None, :], second_part.shape)], 0
        )
    )
    third_part = jax.nn.silu(jnp.einsum("oc,cpv->opv", vfe_three, joined_two, precision=highest))
    return jnp.sum(third_part * valid, axis=1) * inverse


def conv_volume(volume, kernel, stride, pad_depth):
    return lax.conv_general_dilated(
        volume,
        kernel,
        (stride, 1, 1),
        ((pad_depth, pad_depth), (1, 1), (1, 1)),
        dimension_numbers=("NDHWC", "DHWIO", "NDHWC"),
        precision=highest,
    )


def layer_step(volume, kernel):
    return jax.nn.silu(conv_volume(volume, kernel, 1, 0))


def plane_conv(image, kernel, stride):
    return lax.conv_general_dilated(
        image,
        kernel,
        (stride, stride),
        ((1, 1), (1, 1)),
        dimension_numbers=("NHWC", "HWIO", "NHWC"),
        precision=highest,
    )


def upsample(image, kernel):
    factor = kernel.shape[0]
    spread = jnp.einsum("nijc,abco->niajbo", image, kernel, precision=highest)
    return spread.reshape(
        image.shape[0], image.shape[1] * factor, image.shape[2] * factor, kernel.shape[3]
    )


def scene_loss(head_maps, places, anchors, anchor_counts, targets, total_cells):
    scene_count = head_maps.shape[0]
    local_cells = head_maps.shape[2] * head_maps.shape[3]
    flat_maps = head_maps.reshape(scene_count, 16, local_cells)
    logits = flat_maps[:, 0:2]
    live = (jnp.arange(anchors.shape[1], dtype=jnp.int32)[None, :] < anchor_counts[:, None]).astype(
        jnp.float32
    )
    matches = (anchors[:, :, None, None] == places[None, None, :, :]).astype(jnp.float32)
    positive = jnp.sum(matches * live[:, :, None, None], axis=1)
    class_loss = jnp.sum(jax.nn.softplus(logits) - positive * logits) / (2.0 * total_cells)
    boxes = flat_maps[:, 2:16].reshape(scene_count, 2, 7, local_cells)
    goals = targets.reshape(scene_count, 2, 7, local_cells)
    differ = boxes - goals
    magnitude = jnp.abs(differ)
    huber = jnp.where(magnitude < 1.0, 0.5 * differ * differ, magnitude - 0.5)
    weight_pos = positive.reshape(scene_count, 2, 1, local_cells)
    per_scene = jnp.sum(huber * weight_pos, axis=(1, 2, 3)) / jnp.maximum(
        anchor_counts.astype(jnp.float32), 1.0
    )
    return class_loss + jnp.sum(per_scene)


def region_forward(region_kernels, bird_view, anchors, anchor_counts, targets):
    conv_a, conv_b, conv_c, up_a, up_b, up_c, head_kernel = region_kernels
    level_one = rounded(jax.nn.silu(plane_conv(bird_view, conv_a, 2)))
    level_two = rounded(jax.nn.silu(plane_conv(level_one, conv_b, 2)))
    level_three = rounded(jax.nn.silu(plane_conv(level_two, conv_c, 2)))
    joined = rounded(
        jnp.concatenate(
            [
                jax.nn.silu(plane_conv(level_one, up_a, 1)),
                jax.nn.silu(upsample(level_two, up_b)),
                jax.nn.silu(upsample(level_three, up_c)),
            ],
            -1,
        )
    )
    cells = joined.shape[1] * joined.shape[2]
    head_maps = jnp.einsum("nijc,ck->nkij", joined, head_kernel, precision=highest)
    places = (
        jnp.arange(2, dtype=jnp.int32)[:, None] * cells
        + jnp.arange(cells, dtype=jnp.int32)[None, :]
    )
    return (scene_loss(head_maps, places, anchors, anchor_counts, targets, cells), head_maps)


def with_rims(layer_bf):
    return extended(layer_bf, (("slab", 0),), 1)


def send_rims(padded_grad):
    outer = jnp.concatenate([padded_grad[0:1], padded_grad[2:3]], 0)
    arrived = extended(outer.astype(jnp.bfloat16), (("slab", 0),), 1).astype(outer.dtype)
    return round_low(padded_grad[1:2] + arrived[0:1] + arrived[3:4])


def body(
    points,
    point_counts,
    voxel_cells,
    pos_anchors,
    pos_counts,
    reg_targets,
    params,
    moment1,
    moment2,
):
    slab_count = lax.axis_size("slab")
    slab_place = lax.axis_index("slab")
    gathered = lax.all_gather(params.astype(jnp.bfloat16), "slab", axis=0, tiled=True)
    kernels = unpack(gathered.astype(jnp.float32))
    point_cloud = points.astype(jnp.float32)

    def encode(vfe_one, vfe_two, vfe_three, cloud_points):
        return vfe_forward(vfe_one, vfe_two, vfe_three, cloud_points, point_counts)

    features, encode_back = jax.vjp(encode, kernels[0], kernels[1], kernels[2], point_cloud)
    depth_index = voxel_cells // (GY * GX)
    row_index = voxel_cells // GX % GY
    column_index = voxel_cells % GX
    grid_cells = (
        jnp.zeros((2, GY, GX, FC), jnp.float32)
        .at[depth_index, row_index, column_index]
        .set(features.T)
    )
    grid_bf = grid_cells.astype(jnp.bfloat16)
    below = from_behind(grid_bf[1:2], "slab", 1)
    stack_one = jnp.concatenate([below, grid_bf], 0).astype(jnp.float32)[None]
    first_layer, back_one = jax.vjp(layer_step, stack_one, kernels[3])
    stack_two = with_rims(first_layer[0].astype(jnp.bfloat16)).astype(jnp.float32)[None]
    second_layer, back_two = jax.vjp(layer_step, stack_two, kernels[4])
    stack_three = with_rims(second_layer[0].astype(jnp.bfloat16)).astype(jnp.float32)[None]
    third_layer, back_three = jax.vjp(layer_step, stack_three, kernels[5])
    even_mask = (slab_place % 2 == 0).astype(jnp.float32)
    third_bf = (third_layer[0] * even_mask).astype(jnp.bfloat16)
    layers = lax.all_gather(third_bf, "slab", axis=0, tiled=True)
    bird_view = (
        jnp.transpose(layers[0::2], (1, 2, 0, 3)).reshape(1, GY, GX, 2 * C3).astype(jnp.float32)
    )

    def propose(region_kernels, plane):
        return region_forward(region_kernels, plane, pos_anchors, pos_counts, reg_targets)

    loss_value, region_back, full_maps = jax.vjp(propose, kernels[6:], bird_view, has_aux=True)
    region_grads, plane_grad = region_back(jnp.ones_like(loss_value))
    plane_grad = round_low(plane_grad).reshape(GY, GX, 2, C3)
    own_layer_grad = lax.dynamic_index_in_dim(plane_grad, slab_place // 2, 2, False) * even_mask
    layer_cotangent = own_layer_grad[None, None]
    map_share = full_maps.shape[2] // slab_count
    head_maps = lax.dynamic_slice_in_dim(full_maps, slab_place * map_share, map_share, 2)
    region_scale = 1.0 / slab_count
    volume_three, grad_conv_three = back_three(layer_cotangent)
    grad_second = send_rims(volume_three[0])
    volume_two, grad_conv_two = back_two(grad_second[None])
    grad_first = send_rims(volume_two[0])
    volume_one, grad_conv_one = back_one(grad_first[None])
    returned = from_behind(volume_one[0, 0:1].astype(jnp.bfloat16), "slab", -1).astype(jnp.float32)
    grid_grad = round_low(
        volume_one[0, 1:3] + jnp.concatenate([jnp.zeros_like(returned), returned], 0)
    )
    feature_grad = grid_grad[depth_index, row_index, column_index].T
    grad_vfe_one, grad_vfe_two, grad_vfe_three, cloud_grad = encode_back(feature_grad)
    local_grads = [
        grad_vfe_one,
        grad_vfe_two,
        grad_vfe_three,
        grad_conv_one,
        grad_conv_two,
        grad_conv_three,
    ]
    local_grads = local_grads + [piece * region_scale for piece in region_grads]
    flat_grad = jnp.concatenate([piece.reshape(-1) for piece in local_grads])
    shard_length = params.shape[0]
    summed_grads = lax.psum(flat_grad, ("batch", "slab"))
    squares = jnp.sum(summed_grads * summed_grads)
    own_grads = lax.dynamic_slice_in_dim(summed_grads, slab_place * shard_length, shard_length)
    grad_norm = jnp.sqrt(squares)
    clipped = own_grads * (clip_level / jnp.maximum(grad_norm, clip_level))
    new_moment1 = beta_one * moment1 + (1.0 - beta_one) * clipped
    new_moment2 = beta_two * moment2 + (1.0 - beta_two) * clipped * clipped
    direction = (
        new_moment1
        / (1.0 - beta_one**STEP)
        / (jnp.sqrt(new_moment2 / (1.0 - beta_two**STEP)) + adam_eps)
    )
    new_params = params - learn_rate * (direction + weight_decay * params)
    return (head_maps, cloud_grad, new_moment1, new_moment2, new_params, grad_norm)


def solution(mesh):
    in_specs = (
        P(None, None, ("batch", "slab")),
        P(("batch", "slab")),
        P(("batch", "slab")),
        P("batch", None),
        P("batch"),
        P("batch", None, None, None),
        P("slab"),
        P("slab"),
        P("slab"),
    )
    out_specs = (
        P("batch", None, "slab", None),
        P(None, None, ("batch", "slab")),
        P("slab"),
        P("slab"),
        P("slab"),
        P(),
    )
    return jax.shard_map(body, mesh=mesh, in_specs=in_specs, out_specs=out_specs, check_vma=False)
```

profile of v0, /device:TPU:0, one launch (start us, length us, event | category | flops | bytes accessed | tf_op | source)
XLA Modules:
  0.0 1039.6 jit_solution(10771785554110245228)
XLA Ops:
  10.3 2.7 broadcast.413
  13.0 19.8 %dynamic-update-slice = bf16[2537584]{0:T(1024)(128)(2,1)} dynamic-update-slice(bf16[2537584]{0:T(1024)(128)(2,1)} %broadcast.413, bf16[634396]{0:T(1024)(128)(2,1)S(1)} %convert_element_type.193, u32[]{:T(128)} %bitcast.4) | dynamic-update-slice | bytes 2537588
  34.3 185.1 %all-reduce.9.cloned.1.call-done = bf16[2537584]{0:T(1024)(128)(2,1)} async-done(((bf16[2537584]{0:T(1024)(128)(2,1)}), bf16[2537584]{0:T(1024)(128)(2,1)}) %all-reduce.9.cloned.1.call-update) | async-done | bytes 5075184
  222.6 3.7 fusion.111
  227.1 6.7 multiply_reduce_fusion.1
  234.2 30.3 %scatter_fusion = f32[2,32,64,128]{3,2,1,0:T(8,128)S(1)} fusion(f32[2,32,64,128]{3,2,1,0:T(8,128)S(1)} %broadcast_in_dim.42, s32[512]{0:T(512)S(1)} %bitcast.511, f32[512,128]{1,0:T(8,128)S(1)} %copy.511), kind=kCustom, calls=%fused_computation.1 | custom fusion | bytes 792576 | tf_op jit(solution)/shard_map/scatter | solution.py:222
  270.5 8.1 collective-permute-done
  282.1 6.4 add_divide_fusion.4
  290.0 5.2 collective-permute-start.1
  296.7 7.6 collective-permute-done.2
  308.2 4.2 add_divide_fusion.3
  313.8 5.0 collective-permute-start.3
  321.6 5.7 collective-permute-done.4
  331.5 4.2 add_divide_fusion.2
  337.4 2.2 fusion.268
  345.1 3.9 slice.253
  349.0 2.7 reshape.875
  351.7 2.7 copy.624
  364.6 20.7 %all-gather.3.cloned.1.call-done = bf16[4,32,1,64,64]{4,3,2,1,0:T(8,128)(2,1)} async-done(((bf16[1,32,1,64,64]{4,3,2,1,0:T(8,128)(2,1)}), bf16[4,32,1,64,64]{4,3,2,1,0:T(8,128)(2,1)}) %all-gather.3.cloned.1.call-update) | async-done | bytes 1048592 | tf_op jit(solution)/shard_map/all_gather | solution.py:234
  388.9 2.1 reshape.894
  407.6 3.0 add_divide_fusion.6
  423.5 2.1 fusion.123
  425.6 2.2 reshape.555
  429.6 3.0 fusion.72
  434.8 3.2 fusion.39
  445.9 4.2 convolution_multiply_fusion.1
  451.2 2.5 convolution_select_fusion.6
  462.3 2.6 reshape.719
  468.1 38.8 %fusion.11 = f32[3,3,3,64,64]{4,3,2,1,0:T(8,128)S(1)} fusion(f32[1,1,32,64,64]{4,0,3,2,1:T(1,128)S(1)} %bitcast.536, bf16[1,3,32,64,64]{4,2,3,1,0:T(8,128)(2,1)S(1)} %copy-done.28), kind=kOutput, calls=%fused_computation.30 | convolution fusion | flops 2633564160 | bytes 1753088 | tf_op jit(solution)/shard_map/transpose(jvp())/conv_general_dilated | solution.py:105
  511.4 9.8 fusion.271
  526.1 5.3 convolution_multiply_fusion.3
  531.4 3.9 fusion.8
  535.3 5.4 copy.660
  540.7 6.3 copy.739
  550.6 11.0 %fusion.272 = (bf16[3,32,8,9,64]{4,2,3,1,0:T(8,128)(2,1)S(1)}, f32[3,32,8,9,64]{4,2,3,1,0:T(8,128)}) fusion(bf16[3,3,3,64,64]{4,3,2,1,0:T(8,128)(2,1)S(1)} %copy-done.56, f32[1,32,1,7,2,64]{5,3,4,1,2,0:T(8,128)S(1)} %slice.290, f32[1,32,1,8,9,64]{5,3,4,1,2,0:T(8,128)S(1)} %copy.620, pred[8,9]{0,1:T(8,128)(4,1)S(1)} %copy-done.86), kind=kOutput, calls=%fused_computation.442 | convolution fusion | flops 2995372032 | bytes 3579976 | tf_op jit(solution)/shard_map/transpose(jvp())/conv_general_dilated | solution.py:105
  562.7 5.4 collective-permute-start.7
  570.3 38.8 %fusion.13 = f32[3,3,3,64,64]{4,3,2,1,0:T(8,128)S(1)} fusion(bf16[1,3,32,64,64]{4,2,3,1,0:T(8,128)(2,1)S(1)} %copy-done.27, f32[1,1,32,64,64]{4,2,3,1,0:T(8,128)S(1)} %fusion.82), kind=kOutput, calls=%fused_computation.32 | convolution fusion | flops 2633564160 | bytes 1753088 | tf_op jit(solution)/shard_map/transpose(jvp())/conv_general_dilated | solution.py:105
  615.9 8.9 convolution_select_fusion.2
  628.2 44.7 %fusion.9 = f32[3,3,3,128,64]{4,3,2,1,0:T(8,128)} fusion(bf16[1,3,32,64,128]{4,3,2,1,0:T(8,128)(2,1)S(1)} %copy-done.26, f32[1,1,32,64,64]{4,2,3,1,0:T(8,128)S(1)} %fusion.84), kind=kOutput, calls=%fused_computation.28 | convolution fusion | flops 5267128320 | bytes 2981888 | tf_op jit(solution)/shard_map/transpose(jvp())/conv_general_dilated | solution.py:105
  675.8 2.3 fusion.38
  678.8 5.9 gather_fusion
  685.9 13.1 %convolution_bitcast_fusion = f32[16384]{0:T(1024)} fusion(bf16[128,35,512]{2,0,1:T(8,128)(2,1)} %copy-done.5, f32[128,35,512]{2,0,1:T(8,128)} %get-tuple-element.91, f32[128,512]{1,0:T(8,128)S(1)} %copy.633, f32[35,512]{1,0:T(8,128)S(1)} %copy-done.48), kind=kOutput, calls=%fused_computation.38 | convolution fusion | flops 3546152960 | bytes 14161920 | tf_op jit(solution)/shard_map/transpose(jvp(oc,cpv->opv))/dot_general | solution.py:100
  699.0 10.7 %convert_bitcast_fusion = bf16[128,35,512]{2,0,1:T(8,128)(2,1)S(1)} fusion(bf16[2537584]{0:T(1024)(128)(2,1)} %all-reduce.9.cloned.1.call-done, f32[128,35,512]{2,0,1:T(8,128)} %get-tuple-element.91, f32[128,512]{1,0:T(8,128)S(1)} %copy.633, f32[35,512]{1,0:T(8,128)S(1)} %copy-done.48), kind=kOutput, calls=%fused_computation.16 | convolution fusion | flops 3548446720 | bytes 14129152 | tf_op jit(solution)/shard_map/transpose(jvp(oc,cpv->opv))/dot_general | solution.py:100
  713.4 2.2 convolution_bitcast_fusion.4
  720.2 91.9 %concatenate.70 = f32[2537584]{0:T(1024)} concatenate(f32[112]{0:T(128)S(1)} %reshape.562, f32[2048]{0:T(1024)S(1)} %reshape.563, f32[16384]{0:T(1024)} %convolution_bitcast_fusion, f32[221184]{0:T(1024)S(1)} %reshape.565, f32[110592]{0:T(1024)} %reshape.566, f32[110592]{0:T(1024)} %reshape.567, f32[147456]{0:T(1024)} %bitcast.578, f32[147456]{0:T(1024)} %bitcast.577, ...), dimensions={0} | concatenate | bytes 20300672 | tf_op jit(solution)/shard_map/concatenate | solution.py:270
  815.3 200.0 %all-reduce.7.cloned.1.call-done = f32[2537584]{0:T(1024)} async-done(((f32[2537584]{0:T(1024)}), f32[2537584]{0:T(1024)}) %all-reduce.7.cloned.1.call-update) | async-done | bytes 10150352 | tf_op jit(solution)/shard_map/psum | solution.py:272
  1015.3 6.6 multiply_reduce_fusion
  1022.6 8.8 multiply_subtract_fusion
  (454 shorter events, 148.5 us)
Async XLA Ops:
  7.2 213.8 %copy-start = (bf16[7,35,512]{2,1,0:T(8,128)(2,1)S(1)}, bf16[7,35,512]{2,1,0:T(8,128)(2,1)}, u32[]{:S(2)}) copy-start(bf16[7,35,512]{2,1,0:T(8,128)(2,1)} %param.9) | copy-start | bytes 752644
  7.2 212.1 %all-reduce.9.cloned.1.call-start = ((), (), s32[]{:S(2)}) async-start(), calls=%async_computation.2 | async-start | bytes 10153984
  32.8 352.4 %all-gather.3.cloned.1.call-start = ((), (), s32[]{:S(2)}) async-start(), calls=%async_computation.1 | async-start | bytes 2621440 | tf_op jit(solution)/shard_map/all_gather | solution.py:234
  33.6 200.1 %copy-start.66 = (f32[512]{0:T(512)}, f32[512]{0:T(512)S(1)}, u32[]{:S(2)}) copy-start(f32[512]{0:T(512)S(1)} %convert_divide_fusion) | copy-start | bytes 6148
  34.3 192.8 %copy-start.47 = (f32[35,512]{1,0:T(8,128)}, f32[35,512]{1,0:T(8,128)S(1)}, u32[]{:S(2)}) copy-start(f32[35,512]{1,0:T(8,128)S(1)} %fusion.190) | copy-start | bytes 215044
  222.6 3.7 copy-start.6
  227.1 6.7 copy-start.5
  264.5 2.6 copy-start.83
  265.5 13.0 %collective-permute-start = (bf16[1,32,64,128]{3,2,1,0:T(8,128)(2,1)}, bf16[1,32,64,128]{3,2,1,0:T(8,128)(2,1)S(1)}, u32[]{:S(2)}, u32[]{:S(2)}) collective-permute-start(bf16[1,32,64,128]{3,2,1,0:T(8,128)(2,1)} %slice.233), channel_id=1, source_target_pairs={{0,1},{1,2},{2,3},{4,5},{5,6},{6,7},{8,9},{9,10},{10,11},{12,13},{... | collective-permute-start | bytes 1572872 | tf_op jit(solution)/shard_map/ppermute | solution.py:45
  270.5 11.6 %copy-start.45 = (bf16[3,3,3,128,64]{4,3,2,1,0:T(8,128)(2,1)}, bf16[3,3,3,128,64]{4,3,2,1,0:T(8,128)(2,1)S(1)}, u32[]{:S(2)}) copy-start(bf16[3,3,3,128,64]{4,3,2,1,0:T(8,128)(2,1)S(1)} %reshape.536) | copy-start | bytes 1327108
  288.7 15.6 %collective-permute-start.2 = (bf16[1,32,64,64]{3,1,2,0:T(8,128)(2,1)S(1)}, bf16[1,32,64,64]{3,1,2,0:T(8,128)(2,1)S(1)}, u32[]{:S(2)}, u32[]{:S(2)}) collective-permute-start(bf16[1,32,64,64]{3,1,2,0:T(8,128)(2,1)S(1)} %slice_bitcast_fusion.15), channel_id=1, source_target_pairs={{1,0},{2,1},{3,2},{5,4},{6,5},{7,6},{9,8},{10,9},{11,10},{13,12},{... | collective-permute-start | bytes 786440 | tf_op jit(solution)/shard_map/ppermute | solution.py:37
  290.0 15.5 %collective-permute-start.1 = (bf16[1,32,64,64]{3,1,2,0:T(8,128)(2,1)S(1)}, bf16[1,32,64,64]{3,1,2,0:T(8,128)(2,1)S(1)}, u32[]{:S(2)}, u32[]{:S(2)}) collective-permute-start(bf16[1,32,64,64]{3,1,2,0:T(8,128)(2,1)S(1)} %slice_bitcast_fusion.15), channel_id=1, source_target_pairs={{0,1},{1,2},{2,3},{4,5},{5,6},{6,7},{8,9},{9,10},{10,11},{12,13},{... | collective-permute-start | bytes 786440 | tf_op jit(solution)/shard_map/ppermute | solution.py:36
  296.7 11.6 %copy-start.55 = (bf16[3,3,3,64,64]{4,3,2,1,0:T(8,128)(2,1)}, bf16[3,3,3,64,64]{4,3,2,1,0:T(8,128)(2,1)S(1)}, u32[]{:S(2)}) copy-start(bf16[3,3,3,64,64]{4,3,2,1,0:T(8,128)(2,1)S(1)} %reshape.537) | copy-start | bytes 663556
  312.5 14.8 %collective-permute-start.4 = (bf16[1,32,64,64]{3,1,2,0:T(8,128)(2,1)S(1)}, bf16[1,32,64,64]{3,1,2,0:T(8,128)(2,1)S(1)}, u32[]{:S(2)}, u32[]{:S(2)}) collective-permute-start(bf16[1,32,64,64]{3,1,2,0:T(8,128)(2,1)S(1)} %slice_bitcast_fusion.14), channel_id=1, source_target_pairs={{1,0},{2,1},{3,2},{5,4},{6,5},{7,6},{9,8},{10,9},{11,10},{13,12},{... | collective-permute-start | bytes 786440 | tf_op jit(solution)/shard_map/ppermute | solution.py:37
  313.8 14.7 %collective-permute-start.3 = (bf16[1,32,64,64]{3,1,2,0:T(8,128)(2,1)S(1)}, bf16[1,32,64,64]{3,1,2,0:T(8,128)(2,1)S(1)}, u32[]{:S(2)}, u32[]{:S(2)}) collective-permute-start(bf16[1,32,64,64]{3,1,2,0:T(8,128)(2,1)S(1)} %slice_bitcast_fusion.14), channel_id=1, source_target_pairs={{0,1},{1,2},{2,3},{4,5},{5,6},{6,7},{8,9},{9,10},{10,11},{12,13},{... | collective-permute-start | bytes 786440 | tf_op jit(solution)/shard_map/ppermute | solution.py:36
  336.9 678.4 %all-reduce.7.cloned.1.call-start = ((), (), s32[]{:S(2)}) async-start(), calls=%async_computation | async-start | bytes 20307968 | tf_op jit(solution)/shard_map/psum | solution.py:272
  351.6 2.7 copy-start.31
  351.6 3.9 copy-start.30
  395.5 3.9 copy-start.18
  395.5 3.9 copy-start.90
  400.4 3.0 copy-start.73
  404.1 3.5 copy-start.63
  407.6 3.1 copy-start.21
  418.7 3.3 copy-start.51
  427.8 4.8 copy-start.77
  429.6 3.1 copy-start.76
  429.6 3.2 copy-start.75
  434.8 3.2 copy-start.19
  442.5 3.4 copy-start.22
  442.5 3.4 copy-start.54
  451.2 2.6 copy-start.82
  462.3 3.8 copy-start.14
  508.7 2.8 copy-start.58
  508.7 2.8 copy-start.86
  521.5 25.5 %collective-permute-start.5 = (bf16[1,32,64,64]{3,1,2,0:T(8,128)(2,1)S(1)}, bf16[1,32,64,64]{3,1,2,0:T(8,128)(2,1)S(1)}, u32[]{:S(2)}, u32[]{:S(2)}) collective-permute-start(bf16[1,32,64,64]{3,1,2,0:T(8,128)(2,1)S(1)} %slice_bitcast_fusion.12), channel_id=1, source_target_pairs={{0,1},{1,2},{2,3},{4,5},{5,6},{6,7},{8,9},{9,10},{10,11},{12,13},{... | collective-permute-start | bytes 786440 | tf_op jit(solution)/shard_map/ppermute | solution.py:36
  523.5 23.6 %collective-permute-start.6 = (bf16[1,32,64,64]{3,1,2,0:T(8,128)(2,1)S(1)}, bf16[1,32,64,64]{3,1,2,0:T(8,128)(2,1)}, u32[]{:S(2)}, u32[]{:S(2)}) collective-permute-start(bf16[1,32,64,64]{3,1,2,0:T(8,128)(2,1)S(1)} %slice_bitcast_fusion.11), channel_id=1, source_target_pairs={{1,0},{2,1},{3,2},{5,4},{6,5},{7,6},{9,8},{10,9},{11,10},{13,12},{... | collective-permute-start | bytes 786440 | tf_op jit(solution)/shard_map/ppermute | solution.py:37
  526.0 5.3 copy-start.20
  526.0 5.3 copy-start.74
  561.8 8.5 copy-start.27
  562.7 49.4 %collective-permute-start.7 = (bf16[1,32,64,64]{3,1,2,0:T(8,128)(2,1)}, bf16[1,32,64,64]{3,1,2,0:T(8,128)(2,1)}, u32[]{:S(2)}, u32[]{:S(2)}) collective-permute-start(bf16[1,32,64,64]{3,1,2,0:T(8,128)(2,1)} %slice_bitcast_fusion.10), channel_id=1, source_target_pairs={{0,1},{1,2},{2,3},{4,5},{5,6},{6,7},{8,9},{9,10},{10,11},{12,13},{... | collective-permute-start | bytes 786440 | tf_op jit(solution)/shard_map/ppermute | solution.py:36
  569.0 43.1 %collective-permute-start.8 = (bf16[1,32,64,64]{3,1,2,0:T(8,128)(2,1)}, bf16[1,32,64,64]{3,1,2,0:T(8,128)(2,1)}, u32[]{:S(2)}, u32[]{:S(2)}) collective-permute-start(bf16[1,32,64,64]{3,1,2,0:T(8,128)(2,1)} %slice_bitcast_fusion.9), channel_id=1, source_target_pairs={{1,0},{2,1},{3,2},{5,4},{6,5},{7,6},{9,8},{10,9},{11,10},{13,12},{... | collective-permute-start | bytes 786440 | tf_op jit(solution)/shard_map/ppermute | solution.py:37
  624.8 3.4 copy-start.26
  626.8 49.0 %collective-permute-start.9 = (bf16[1,32,64,128]{3,2,1,0:T(8,128)(2,1)}, bf16[1,32,64,128]{3,2,1,0:T(8,128)(2,1)}, u32[]{:S(2)}, u32[]{:S(2)}) collective-permute-start(bf16[1,32,64,128]{3,2,1,0:T(8,128)(2,1)} %bitcast.503), channel_id=1, source_target_pairs={{1,0},{2,1},{3,2},{5,4},{6,5},{7,6},{9,8},{10,9},{11,10},{13,12},{... | collective-permute-start | bytes 1572872 | tf_op jit(solution)/shard_map/ppermute | solution.py:45
  678.4 6.3 copy-start.67
  678.4 7.5 copy-start.48
  685.9 25.5 %slice-start.1 = ((s8[4587520]{0:T(1024)(128)(4,1)}), s8[4194304]{0:T(1024)(128)(4,1)S(1)}, s32[]{:S(2)}) async-start(s8[4587520]{0:T(1024)(128)(4,1)} %bitcast.523), calls=%async_computation.4 | async-start | bytes 8388608
  699.0 12.4 %slice-start.2 = ((s8[4587520]{0:T(1024)(128)(4,1)}), s8[393216]{0:T(1024)(128)(4,1)S(1)}, s32[]{:S(2)}) async-start(s8[4587520]{0:T(1024)(128)(4,1)} %bitcast.523), calls=%async_computation.5 | async-start | bytes 786432
  815.3 207.3 %copy-start.2 = (f32[634396]{0:T(1024)S(1)}, f32[634396]{0:T(1024)}, u32[]{:S(2)}) copy-start(f32[634396]{0:T(1024)} %param.15) | copy-start | bytes 7612756
  (60 other events, 94.6 us)
Sparse Core Ops, SparseCore 0:
  32.9 186.3 all-reduce.8
  337.0 48.1 all-gather.2
  812.2 203.0 all-reduce.6
where the time goes:
time: 1050 us; the launch traced here: 1040 us
  waiting for transfers between devices  430 us (41%)
  local copies, waits for them, and re-layouts  273 us (26%)
  matrix products  249 us (24%)
  other arithmetic  42.1 us (4%)
  starting transfers between devices  26.1 us (2%)
  between operations  19.8 us (2%)
    psum x1, waiting for transfers between devices, body(): summed_grads = lax.psum(flat_grad, ('batch', 'slab'))  200 us
    unnamed x4, waiting for transfers between devices  185 us
    conv_general_dilated x9, matrix products, conv_volume(): lax.conv_general_dilated(volume, kernel, (stride, 1, 1), ((pad_depth, pad...  167 us
    concatenate x1, local copies, waits for them, and re-layouts, body(): flat_grad = jnp.concatenate([piece.reshape(-1) for piece in local_grads])  91.9 us
    unnamed x205, local copies, waits for them, and re-layouts  49.8 us
    dot_general x3, matrix products, vfe_forward(): jnp.einsum('oc,cpv->opv', vfe_three, joined_two, precision=highest)  30.5 us
    scatter x1, local copies, waits for them, and re-layouts, body(): grid_cells = jnp.zeros((2, GY, GX, FC), jnp.float32).at[depth_index, row_...  30.3 us
    conv_general_dilated x12, matrix products, plane_conv(): lax.conv_general_dilated(image, kernel, (stride, stride), ((1, 1), (1, 1)...  25.4 us
  transfers between devices with their start and end apart: 13, of which 8 were waited for; matrix products, arithmetic and copies ran while one was open for 14% of the time, Pallas kernels for 0%

commit v1 on v0

v1 whole, which is shorter than its diff:
```python
import functools
import math

import jax
import jax.numpy as jnp
from jax import lax
from jax.experimental import pallas as pl
from jax.experimental.pallas import tpu as pltpu
from jax.sharding import PartitionSpec as P

VF1 = 16
VF2 = 64
FC = 128
C3 = 64
STEP = 10
GY = 32
GX = 64
PTS = 35
VOX = 512
SLABS = 4
ROWS = GY // SLABS
LANES = 128
NPARAM = 2537584
SHARD = NPARAM // SLABS

TILE = 16
STRIDE_T = 310
SHARD_T = 312
PAD_T = 320
FLAT_R = 4960
CONV_R0 = 144
CONV_R = 3456
PLANE_T0 = 225
PLANE_T = 1014
GRAD_T = 3 * STRIDE_T + SHARD_T
WIDE_T = (369, 1233)
CONV_T = 256

beta_one = 0.9
beta_two = 0.999
adam_eps = 1e-08
learn_rate = 0.02
weight_decay = 0.01
clip_level = 0.002

f32 = jnp.float32
bf16 = jnp.bfloat16
VMEM_LIMIT = 56 * 1024 * 1024


def call(kernel, out_shape, in_specs, out_specs, scratch=()):
    return pl.pallas_call(
        kernel,
        out_shape=out_shape,
        in_specs=in_specs,
        out_specs=out_specs,
        scratch_shapes=list(scratch),
        compiler_params=pltpu.CompilerParams(vmem_limit_bytes=VMEM_LIMIT),
    )


def vmem():
    return pl.BlockSpec(memory_space=pltpu.VMEM)


def smem():
    return pl.BlockSpec(memory_space=pltpu.SMEM)


def anywhere():
    return pl.BlockSpec(memory_space=pl.ANY)


def shape(dims, dtype=f32):
    return jax.ShapeDtypeStruct(dims, dtype)


def mm(a, b):
    return lax.dot_general(a, b, (((1,), (0,)), ((), ())), preferred_element_type=f32)


def mm_nt(a, b):
    return lax.dot_general(a, b, (((1,), (1,)), ((), ())), preferred_element_type=f32)


def mm_tn(a, b):
    return lax.dot_general(a, b, (((0,), (0,)), ((), ())), preferred_element_type=f32)


def sigmoid(z):
    return 0.5 * jnp.tanh(0.5 * z) + 0.5


def silu(z):
    return z * sigmoid(z)


def silu_slope(z):
    s = sigmoid(z)
    return s * (1.0 + z * (1.0 - s))


def lane_of(dims):
    return lax.broadcasted_iota(jnp.int32, dims, len(dims) - 1)


def row_of(dims):
    return lax.broadcasted_iota(jnp.int32, dims, 0)


def lane_roll(x, shift):
    shift = shift % x.shape[-1]
    return x if shift == 0 else pltpu.roll(x, shift, x.ndim - 1)


def shift_in(v, d, width):
    if d == 0:
        return v
    place = row_of(v.shape) % width
    keep = place > 0 if d > 0 else place < width - 1
    return jnp.where(keep, pltpu.roll(v, d % v.shape[0], 0), 0.0)


def shift_out(v, d, width):
    if d == 0:
        return v
    edge = jnp.zeros((width,) + v.shape[1:], v.dtype)
    if d > 0:
        return jnp.concatenate([edge, v[:-width]], 0)
    return jnp.concatenate([v[width:], edge], 0)


def spread_kernel(slab_ref, flat_ref, out_ref, nat):
    nat[...] = jnp.zeros_like(nat)
    span = 480
    for s in range(SLABS):

        @pl.when(slab_ref[0] == s)
        def _(s=s):
            lanes, first = 16 + 28 * s, 15 - 4 * s
            lane = lane_of((span, LANES))
            count = FLAT_R // span + (FLAT_R % span > 0)
            for i in range(count):
                r0 = i * span
                n = min(span, FLAT_R - r0)
                rolled = lane_roll(flat_ref[r0 : r0 + n, :], lanes)
                nat[first + r0 : first + r0 + n, :] += jnp.where(lane[:n] >= lanes, rolled, 0.0)
                nat[first + r0 + 1 : first + r0 + 1 + n, :] += jnp.where(
                    lane[:n] < lanes, rolled, 0.0
                )
            low = max(0, min(SHARD_T // 2, (WIDE_T[0] - STRIDE_T * s + 1) // 2))
            high = max(low, min(SHARD_T // 2, (WIDE_T[1] - STRIDE_T * s + 1) // 2))
            for a, b, wide in ((0, low, False), (low, high, True), (high, SHARD_T // 2, False)):

                def block(i, carry, wide=wide):
                    base = pl.multiple_of(32 * i, 32)
                    if wide:
                        even = nat[pl.ds(base, 16, stride=2), :]
                        odd = nat[pl.ds(base + 1, 16, stride=2), :]
                    else:
                        even = nat[pl.ds(base, 16), :]
                        odd = nat[pl.ds(base + 16, 16), :]
                    out_ref[2 * i] = even.astype(bf16)
                    out_ref[2 * i + 1] = odd.astype(bf16)
                    return carry

                if b > a:
                    lax.fori_loop(a, b, block, 0, unroll=4)

    for t in range(SHARD_T, PAD_T):
        out_ref[t] = jnp.zeros((TILE, LANES), bf16)


def spread_shard(slab, flat_rows):
    return call(
        spread_kernel,
        shape((PAD_T, TILE, LANES), bf16),
        [smem(), vmem()],
        vmem(),
        [pltpu.VMEM((5120, LANES), f32)],
    )(slab, flat_rows)


def gather_kernel(slab_ref, quarter_ref, early_ref, out_ref, squares_ref, nat):
    span = 480
    for s in range(SLABS):

        @pl.when(slab_ref[0] == s)
        def _(s=s):
            lanes, first = 16 + 28 * s, 15 - 4 * s
            low = max(0, min(SHARD_T // 2, (WIDE_T[0] - STRIDE_T * s + 1) // 2))
            high = max(low, min(SHARD_T // 2, (WIDE_T[1] - STRIDE_T * s + 1) // 2))
            for a, b, wide in ((0, low, False), (low, high, True), (high, SHARD_T // 2, False)):

                def block(i, carry, wide=wide):
                    base = pl.multiple_of(32 * i, 32)
                    even, odd = quarter_ref[2 * i], quarter_ref[2 * i + 1]
                    if wide:
                        nat[pl.ds(base, 16, stride=2), :] = even
                        nat[pl.ds(base + 1, 16, stride=2), :] = odd
                    else:
                        nat[pl.ds(base, 16), :] = even
                        nat[pl.ds(base + 16, 16), :] = odd
                    return carry

                if b > a:
                    lax.fori_loop(a, b, block, 0, unroll=4)
            if s == 0:
                rows = CONV_R + CONV_R0 + TILE
                nat[0:rows, :] = early_ref[0:rows, :].astype(f32)
            lane = lane_of((span, LANES))
            total = jnp.zeros((8, LANES), f32)
            count = FLAT_R // span + (FLAT_R % span > 0)
            for i in range(count):
                r0 = i * span
                n = min(span, FLAT_R - r0)
                here = lane_roll(nat[first + r0 : first + r0 + n, :], -lanes)
                after = lane_roll(nat[first + r0 + 1 : first + r0 + 1 + n, :], -lanes)
                value = jnp.where(lane[:n] < LANES - lanes, here, after)
                if r0 + n > SHARD // LANES:
                    place = (row_of((n, LANES)) + r0) * LANES + lane[:n]
                    value = jnp.where(place < SHARD, value, 0.0)
                out_ref[r0 : r0 + n, :] = value
                total += jnp.sum((value * value).reshape(n // 8, 8, LANES), axis=0)
            squares_ref[...] = total


def gather_shard(slab, quarter, early):
    return call(
        gather_kernel,
        (shape((FLAT_R, LANES)), shape((8, LANES))),
        [smem(), vmem(), vmem()],
        (vmem(), vmem()),
        [pltpu.VMEM((5120, LANES), f32)],
    )(slab, quarter, early)


PART = 5
VFE_SCRATCH = [
    pltpu.VMEM((VOX // LANES, PTS * 16, LANES), f32),
    pltpu.VMEM((16, LANES), f32),
    pltpu.VMEM((64, LANES), f32),
    pltpu.VMEM((PTS * 16, VOX), bf16),
    pltpu.VMEM((PTS * 64, VOX), bf16),
]


def spread_points(points_ref, x_scr):
    x_scr[...] = jnp.zeros_like(x_scr)
    for c in range(7):
        plane = points_ref[c].astype(f32)
        for b in range(VOX // LANES):
            x_scr[b, pl.ds(c, PTS, stride=16), :] = plane[:, b * LANES : (b + 1) * LANES]


def vfe_weights(rows_ref, w1_scr, w2_scr):
    line = rows_ref[0].astype(f32)
    lane = lane_of((16, LANES))
    for o in range(VF1):
        w1_scr[o : o + 1, :] = jnp.where(lane < 7, lane_roll(line, -(16 + 7 * o)), 0.0)[15:16]
    two = rows_ref[1].astype(f32)
    for k in range(4):
        w2_scr[pl.ds(k, 16, stride=4), :] = jnp.where(lane < 32, lane_roll(two, -32 * k), 0.0)
    w1 = w1_scr[...].astype(bf16)[:, 0:16]
    w2 = w2_scr[...]
    w2a = w2.astype(bf16)[:, 0:16]
    w2b = lane_roll(w2, -16).astype(bf16)[:, 0:16]
    w3 = rows_ref[2:10].reshape(FC, LANES)
    w3a = w3[:, 0:64]
    w3b = lane_roll(w3.astype(f32), -64).astype(bf16)[:, 0:64]
    return w1, w2a, w2b, w3a, w3b


def part_of(ref, i, height):
    return jnp.concatenate(
        [
            ref[pl.ds(pl.multiple_of((PART * i + k) * height, height), height), :]
            for k in range(PART)
        ],
        1,
    )


def points_part(ref, i):
    return jnp.concatenate(
        [
            ref[b, pl.ds(pl.multiple_of((PART * i + k) * 16, 16), 16), :]
            for k in range(PART)
            for b in range(VOX // LANES)
        ],
        1,
    )


def set_points_part(ref, i, value):
    for k in range(PART):
        for b in range(VOX // LANES):
            at = k * VOX + b * LANES
            ref[b, pl.ds(pl.multiple_of((PART * i + k) * 16, 16), 16), :] = value[:, at : at + LANES]


def set_part(ref, i, height, value):
    for k in range(PART):
        ref[pl.ds(pl.multiple_of((PART * i + k) * height, height), height), :] = value[
            :, k * VOX : (k + 1) * VOX
        ].astype(ref.dtype)


def part_sum(value):
    total = value[:, 0:VOX]
    for k in range(1, PART):
        total = total + value[:, k * VOX : (k + 1) * VOX]
    return total


def valid_part(i, counts):
    return jnp.concatenate([(PART * i + k < counts).astype(f32) for k in range(PART)], 1)


def widen(value):
    return jnp.concatenate([value] * PART, 1)


def vfe_front(weights, counts, inverse, x_scr, j1_scr, j2_scr, z1_scr=None, z2_scr=None):
    w1, w2a, w2b, w3a, w3b = weights

    def layer_one(i, total):
        z = mm(w1, points_part(x_scr, i).astype(bf16))
        value = silu(z)
        set_part(j1_scr, i, 16, value)
        if z1_scr is not None:
            set_part(z1_scr, i, 16, z)
        return total + part_sum(value * valid_part(i, counts))

    total = lax.fori_loop(0, PTS // PART, layer_one, jnp.zeros((VF1, VOX), f32))
    mean_one = (total * inverse).astype(bf16)
    shared_two = widen(mm(w2b, mean_one))

    def layer_two(i, total):
        z = mm(w2a, part_of(j1_scr, i, 16)) + shared_two
        value = silu(z)
        set_part(j2_scr, i, 64, value)
        if z2_scr is not None:
            set_part(z2_scr, i, 64, z)
        return total + part_sum(value * valid_part(i, counts))

    total = lax.fori_loop(0, PTS // PART, layer_two, jnp.zeros((VF2, VOX), f32))
    mean_two = (total * inverse).astype(bf16)
    shared_three = widen(mm(w3b, mean_two))
    return mean_one, mean_two, shared_three


def encode_kernel(points_ref, counts_ref, cells_ref, rows_ref, out_ref, x_scr, w1_scr, w2_scr, j1_scr, j2_scr):
    spread_points(points_ref, x_scr)
    weights = vfe_weights(rows_ref, w1_scr, w2_scr)
    counts = counts_ref[...]
    inverse = 1.0 / counts.astype(f32)
    _, _, shared_three = vfe_front(weights, counts, inverse, x_scr, j1_scr, j2_scr)
    w3a = weights[3]

    def layer_three(i, total):
        value = silu(mm(w3a, part_of(j2_scr, i, 64)) + shared_three)
        return total + part_sum(value * valid_part(i, counts))

    total = lax.fori_loop(0, PTS // PART, layer_three, jnp.zeros((FC, VOX), f32))
    out_ref[0:FC, :] = (total * inverse).astype(bf16)
    cells = cells_ref[...]
    row = row_of((16, VOX))
    high, low = cells // GX, cells % GX
    out_ref[FC : FC + 16, :] = jnp.where(row == 0, high, low).astype(f32).astype(bf16)


def encode(points, counts, cells, rows):
    return call(
        encode_kernel,
        shape((FC + 16, VOX), bf16),
        [vmem()] * 4,
        vmem(),
        VFE_SCRATCH,
    )(points, counts, cells, rows)


def encode_back_kernel(
    points_ref, counts_ref, rows_ref, grad_ref, out_ref, weight_ref,
    x_scr, w1_scr, w2_scr, j1_scr, j2_scr, z1_scr, z2_scr, d1_scr, d2_scr,
):
    spread_points(points_ref, x_scr)
    weights = vfe_weights(rows_ref, w1_scr, w2_scr)
    w1, w2a, w2b, w3a, w3b = weights
    counts = counts_ref[...]
    inverse = 1.0 / counts.astype(f32)
    mean_one, mean_two, shared_three = vfe_front(
        weights, counts, inverse, x_scr, j1_scr, j2_scr, z1_scr, z2_scr
    )
    grad = grad_ref[0].astype(f32)
    for t in range(1, SLABS):
        grad = grad + grad_ref[t].astype(f32)
    grad_three = widen(grad * inverse)
    parts = PTS // PART

    def back_three(i, carry):
        total, weight = carry
        j2 = part_of(j2_scr, i, 64)
        z = mm(w3a, j2) + shared_three
        dz = grad_three * valid_part(i, counts) * silu_slope(z)
        low = dz.astype(bf16)
        set_part(d2_scr, i, 64, mm_tn(w3a, low))
        return total + part_sum(dz), weight + mm_nt(low, j2)

    total, grad_w3a = lax.fori_loop(
        0, parts, back_three, (jnp.zeros((FC, VOX), f32), jnp.zeros((FC, VF2), f32))
    )
    total = total.astype(bf16)
    grad_w3b = mm_nt(total, mean_two)
    grad_two = widen(mm_tn(w3b, total) * inverse)

    def back_two(i, carry):
        total, weight = carry
        dz = (part_of(d2_scr, i, 64) + valid_part(i, counts) * grad_two) * silu_slope(
            part_of(z2_scr, i, 64)
        )
        low = dz.astype(bf16)
        set_part(d1_scr, i, 16, mm_tn(w2a, low))
        return total + part_sum(dz), weight + mm_nt(low, part_of(j1_scr, i, 16))

    total, grad_w2a = lax.fori_loop(
        0, parts, back_two, (jnp.zeros((VF2, VOX), f32), jnp.zeros((VF2, VF1), f32))
    )
    total = total.astype(bf16)
    grad_w2b = mm_nt(total, mean_one)
    grad_one = widen(mm_tn(w2b, total) * inverse)

    def back_one(i, weight):
        dz = (part_of(d1_scr, i, 16) + valid_part(i, counts) * grad_one) * silu_slope(
            part_of(z1_scr, i, 16)
        )
        low = dz.astype(bf16)
        x = points_part(x_scr, i).astype(bf16)
        set_points_part(x_scr, i, mm_tn(w1, low))
        return weight + mm_nt(low, x)

    grad_w1 = lax.fori_loop(0, parts, back_one, jnp.zeros((VF1, 16), f32))
    for c in range(7):
        for b in range(VOX // LANES):
            out_ref[c, :, b * LANES : (b + 1) * LANES] = x_scr[b, pl.ds(c, PTS, stride=16), :]

    lane = lane_of((16, LANES))
    w1_scr[...] = jnp.concatenate([grad_w1, jnp.zeros((16, LANES - 16), f32)], 1)
    spread = jnp.where(lane < 7, w1_scr[...], 0.0)
    line = jnp.zeros((16, LANES), f32)
    row = row_of((16, LANES))
    for o in range(VF1):
        line = line + jnp.where(row == o, lane_roll(spread, 16 + 7 * o), 0.0)
    line = jnp.sum(line, axis=0, keepdims=True)
    weight_ref[0:16, :] = jnp.where(row == 15, line, 0.0)
    w2_scr[...] = jnp.concatenate([grad_w2a, grad_w2b, jnp.zeros((64, LANES - 32), f32)], 1)
    two = jnp.zeros((16, LANES), f32)
    for k in range(4):
        two = two + lane_roll(w2_scr[pl.ds(k, 16, stride=4), :], 32 * k)
    weight_ref[16:32, :] = two
    weight_ref[32:160, :] = jnp.concatenate([grad_w3a, grad_w3b], 1)


def encode_back(points, counts, rows, grad):
    return call(
        encode_back_kernel,
        (shape((7, PTS, VOX)), shape((160, LANES))),
        [vmem()] * 4,
        (vmem(), vmem()),
        VFE_SCRATCH
        + [
            pltpu.VMEM((PTS * 16, VOX), f32),
            pltpu.VMEM((PTS * 64, VOX), f32),
            pltpu.VMEM((PTS * 16, VOX), f32),
            pltpu.VMEM((PTS * 64, VOX), f32),
        ],
    )(points, counts, rows, grad)


R1W = (ROWS + 4) * GX
R2W = (ROWS + 2) * GX
R3W = ROWS * GX
RGW = (ROWS + 6) * GX


def cell_marks(places):
    value = places.astype(f32)
    high, low = value[0:1], value[1:2]
    column = lax.broadcasted_iota(jnp.int32, (GX, VOX), 0).astype(f32)
    return (column == low).astype(f32).astype(bf16), high


def layer_marks(column, high, depth, first_row):
    pieces = []
    for w in range(ROWS + 6):
        row = first_row - 3 + w
        inside = jnp.logical_and(row >= 0, row < GY)
        target = jnp.where(inside, depth * GY + row, -1).astype(f32)
        pieces.append(column * (high == target).astype(f32).astype(bf16))
    return jnp.concatenate(pieces, 0)


def conv_weights(rows_ref, start, taps, half, place, scr):
    lane = lane_of((half, LANES))
    left = lane < 64
    for t in range(taps):
        r = []
        for kx in range(3):
            base = start + (3 * t + kx) * half
            r.append(rows_ref[base : base + half, :].astype(f32))
        turned = [lane_roll(v, 64) for v in r]
        at = place(t)
        scr[0, pl.ds(at, half, stride=2), :] = jnp.where(left, r[1], turned[0])
        scr[0, pl.ds(at + 1, half, stride=2), :] = jnp.where(left, turned[1], r[0])
        scr[1, pl.ds(at, half, stride=2), :] = jnp.where(left, r[2], 0.0)
        scr[1, pl.ds(at + 1, half, stride=2), :] = jnp.where(left, turned[2], 0.0)


def conv_weight_grads(out_ref, start, taps, half, place, scr):
    lane = lane_of((half, LANES))
    left = lane < 64
    for t in range(taps):
        at = place(t)
        even = [scr[b, pl.ds(at, half, stride=2), :] for b in range(2)]
        odd = [scr[b, pl.ds(at + 1, half, stride=2), :] for b in range(2)]
        values = (
            jnp.where(left, lane_roll(even[0], 64), odd[0]),
            jnp.where(left, even[0], lane_roll(odd[0], 64)),
            jnp.where(left, even[1], lane_roll(odd[1], 64)),
        )
        for kx in range(3):
            base = start + (3 * t + kx) * half
            out_ref[base : base + half, :] = values[kx]


def both_halves(out_ref, scr):
    for b in range(2):
        out_ref[:, b * LANES : (b + 1) * LANES] = scr[b].astype(bf16)


def keep_halves(scr, value):
    for b in range(2):
        scr[b] = value[:, b * LANES : (b + 1) * LANES]


def tap_place(t):
    return 128 * t


def pair_place(t):
    kd, ky = t // 3, t % 3
    return 128 * ky + 64 * kd if kd < 2 else 384 + 128 * ky


def join_columns(p):
    first, last = p[:, 0:128], p[:, 128:256]
    left = lane_of(first.shape) < 64
    half = jnp.where(left, first + shift_in(last, -1, GX), shift_in(first, 1, GX))
    return half + lane_roll(half, 64)


def split_columns(d):
    left = lane_of(d.shape) < 64
    first = jnp.where(left, d, lane_roll(shift_in(d, -1, GX), 64))
    last = jnp.where(left, shift_in(d, 1, GX), 0.0)
    return jnp.concatenate([first, last], 1).astype(bf16)


def inside_rows(rows, first_row):
    place = first_row + row_of((rows, LANES)) // GX
    return jnp.logical_and(place >= 0, place < GY)


def grid_taps(grid_ref, k):
    return jnp.concatenate(
        [grid_ref[2 * k + kd, ky * GX : ky * GX + R1W, :] for kd in range(3) for ky in range(3)], 1
    )


def pair_taps(ref, at, rows):
    return jnp.concatenate(
        [ref[at, ky * GX : ky * GX + rows, :] for ky in range(3)]
        + [ref[at + 2, ky * GX : ky * GX + rows, :] for ky in range(3)],
        1,
    )


def volume_kernel(
    slab_ref, f_ref, rows_ref,
    bird_ref, grid_ref, first_ref, second_ref, z1_ref, z2_ref, z3_ref, w1_ref, w2_ref, w3_ref,
    w1_scr, w2_scr, bird_scr,
):
    w2_scr[...] = jnp.zeros_like(w2_scr)
    conv_weights(rows_ref, 0, 9, 64, tap_place, w1_scr)
    both_halves(w1_ref, w1_scr)
    conv_weights(rows_ref, 1728, 9, 32, pair_place, w2_scr)
    both_halves(w2_ref, w2_scr)
    conv_weights(rows_ref, 2592, 9, 32, pair_place, w2_scr)
    both_halves(w3_ref, w2_scr)

    first_row = slab_ref[0] * ROWS
    grid_ref[0] = jnp.zeros((RGW, FC), bf16)
    for t in range(SLABS):
        features = f_ref[t, 0:FC, :]
        column, high = cell_marks(f_ref[t, FC : FC + 16, :])
        for d in range(2):
            marks = layer_marks(column, high, d, first_row)
            grid_ref[1 + 2 * t + d] = mm_nt(marks, features).astype(bf16)

    first_ref[0] = jnp.zeros((R1W, LANES), bf16)
    first_ref[5] = jnp.zeros((R1W, LANES), bf16)
    keep = inside_rows(R1W, first_row - 2)
    for k in range(4):
        z = join_columns(mm(grid_taps(grid_ref, k), w1_ref[...]))
        z1_ref[k] = z
        value = jnp.where(keep, silu(z), 0.0).astype(bf16)
        first_ref[k + 1, :, 0:64] = value[:, 0:64]
        first_ref[k, :, 64:128] = value[:, 64:128]
    first_ref[4, :, 64:128] = jnp.zeros((R1W, 64), bf16)

    second_ref[0] = jnp.zeros((R2W, LANES), bf16)
    second_ref[5] = jnp.zeros((R2W, LANES), bf16)
    keep = inside_rows(R2W, first_row - 1)
    for k in range(4):
        z = join_columns(mm(pair_taps(first_ref, k, R2W), w2_ref[...]))
        z2_ref[k] = z
        value = jnp.where(keep, silu(z), 0.0).astype(bf16)
        second_ref[k + 1, :, 0:64] = value[:, 0:64]
        second_ref[k, :, 64:128] = value[:, 64:128]
    second_ref[4, :, 64:128] = jnp.zeros((R2W, 64), bf16)

    z3 = []
    for k in range(2):
        z3.append(join_columns(mm(pair_taps(second_ref, 2 * k, R3W), w3_ref[...])))
    z = jnp.where(lane_of((R3W, LANES)) < 64, z3[0], z3[1])
    z3_ref[...] = z
    bird_scr[...] = silu(z)
    for yp in range(2):
        for xp in range(2):
            for a in range(ROWS // 2):
                piece = bird_scr[pl.ds((2 * a + yp) * GX + xp, GX // 2, stride=2), :]
                bird_ref[2 * yp + xp, a * 32 : a * 32 + 32, :] = piece.astype(bf16)


def volume(slab, features, rows):
    return call(
        volume_kernel,
        (
            shape((4, 128, LANES), bf16),
            shape((9, RGW, LANES), bf16),
            shape((6, R1W, LANES), bf16),
            shape((6, R2W, LANES), bf16),
            shape((4, R1W, LANES)),
            shape((4, R2W, LANES)),
            shape((R3W, LANES)),
            shape((1152, 256), bf16),
            shape((768, 256), bf16),
            shape((768, 256), bf16),
        ),
        [smem(), vmem(), vmem()],
        (vmem(),) * 10,
        [pltpu.VMEM((2, 1152, LANES), f32), pltpu.VMEM((2, 768, LANES), f32), pltpu.VMEM((R3W, LANES), f32)],
    )(slab, features, rows)


def volume_back_kernel(
    slab_ref, f_ref, bird_ref, grid_ref, first_ref, second_ref, z1_ref, z2_ref, z3_ref, w1_ref, w2_ref, w3_ref,
    out_ref, weight_ref,
    bird_scr, acc2, acc1, accg, g1_scr, g2_scr,
):
    first_row = slab_ref[0] * ROWS
    for yp in range(2):
        for xp in range(2):
            for a in range(ROWS // 2):
                piece = bird_ref[2 * yp + xp, a * 32 : a * 32 + 32, :].astype(f32)
                bird_scr[pl.ds((2 * a + yp) * GX + xp, GX // 2, stride=2), :] = piece
    dz = bird_scr[...] * silu_slope(z3_ref[...])
    acc2[...] = jnp.zeros_like(acc2)
    acc1[...] = jnp.zeros_like(acc1)
    accg[...] = jnp.zeros_like(accg)

    def pair_back(acc, at, rows, spread, weight):
        back = mm_nt(spread, weight)
        for ky in range(3):
            acc[at, ky * GX : ky * GX + rows, :] += back[:, 128 * ky : 128 * ky + 128]
            acc[at + 2, ky * GX : ky * GX + rows, :] += back[:, 384 + 128 * ky : 512 + 128 * ky]

    def layer_grad(acc, m):
        return acc[m] + lane_roll(acc[m - 1], 64)

    total = jnp.zeros((768, 256), f32)
    for k in range(2):
        spread = split_columns(dz if k == 0 else lane_roll(dz, 64))
        total = total + mm_tn(pair_taps(second_ref, 2 * k, R3W), spread)
        pair_back(acc2, 2 * k, R3W, spread, w3_ref[...])
    keep_halves(g2_scr, total)
    conv_weight_grads(weight_ref, 2592, 9, 32, pair_place, g2_scr)

    keep = inside_rows(R2W, first_row - 1)
    total = jnp.zeros((768, 256), f32)
    for k in range(4):
        d = jnp.where(keep, layer_grad(acc2, k + 1) * silu_slope(z2_ref[k]), 0.0)
        spread = split_columns(d)
        total = total + mm_tn(pair_taps(first_ref, k, R2W), spread)
        pair_back(acc1, k, R2W, spread, w2_ref[...])
    keep_halves(g2_scr, total)
    conv_weight_grads(weight_ref, 1728, 9, 32, pair_place, g2_scr)

    keep = inside_rows(R1W, first_row - 2)
    total = jnp.zeros((1152, 256), f32)
    for k in range(4):
        d = jnp.where(keep, layer_grad(acc1, k + 1) * silu_slope(z1_ref[k]), 0.0)
        spread = split_columns(d)
        total = total + mm_tn(grid_taps(grid_ref, k), spread)
        back = mm_nt(spread, w1_ref[...])
        for kd in range(3):
            for ky in range(3):
                t = 3 * kd + ky
                accg[2 * k + kd, ky * GX : ky * GX + R1W, :] += back[:, 128 * t : 128 * t + 128]
    keep_halves(g1_scr, total)
    conv_weight_grads(weight_ref, 0, 9, 64, tap_place, g1_scr)

    for t in range(SLABS):
        column, high = cell_marks(f_ref[t, FC : FC + 16, :])
        value = jnp.zeros((FC, VOX), f32)
        for d in range(2):
            marks = layer_marks(column, high, d, first_row)
            value = value + mm_tn(accg[1 + 2 * t + d].astype(bf16), marks)
        out_ref[t] = value.astype(bf16)


def volume_back(slab, features, bird_grad, kept):
    return call(
        volume_back_kernel,
        (shape((SLABS, FC, VOX), bf16), shape((CONV_R, LANES))),
        [smem()] + [vmem()] * 11,
        (vmem(), vmem()),
        [
            pltpu.VMEM((R3W, LANES), f32),
            pltpu.VMEM((6, R2W, LANES), f32),
            pltpu.VMEM((6, R1W, LANES), f32),
            pltpu.VMEM((9, RGW, LANES), f32),
            pltpu.VMEM((2, 1152, LANES), f32),
            pltpu.VMEM((2, 768, LANES), f32),
        ],
    )(slab, features, bird_grad, *kept)


def split_planes(ref, height, width):
    planes = []
    for yp in range(2):
        for xp in range(2):
            planes.append(
                jnp.concatenate(
                    [
                        ref[pl.ds((2 * a + yp) * width + xp, width // 2, stride=2), :]
                        for a in range(height // 2)
                    ],
                    0,
                )
            )
    return planes


def merge_planes(ref, planes, height, width):
    half = width // 2
    for yp in range(2):
        for xp in range(2):
            for a in range(height // 2):
                ref[pl.ds((2 * a + yp) * width + xp, half, stride=2), :] = planes[2 * yp + xp][
                    a * half : a * half + half
                ]


def stride_taps(planes, width):
    pieces = []
    for ky in range(3):
        for kx in range(3):
            v = planes[2 * (ky != 1) + (kx != 1)]
            v = shift_in(v, 1, width) if kx == 0 else v
            pieces.append((shift_out(v, 1, width) if ky == 0 else v).astype(bf16))
    return jnp.concatenate(pieces, 1)


def stride_taps_back(grad, width):
    planes = [None] * 4
    channels = grad.shape[1] // 9
    for ky in range(3):
        for kx in range(3):
            t = 3 * ky + kx
            v = grad[:, t * channels : (t + 1) * channels]
            v = shift_out(v, -1, width) if ky == 0 else v
            v = shift_in(v, -1, width) if kx == 0 else v
            at = 2 * (ky != 1) + (kx != 1)
            planes[at] = v if planes[at] is None else planes[at] + v
    return planes


def full_taps(v, width):
    across = [shift_in(v, 1 - kx, width).astype(bf16) for kx in range(3)]
    return jnp.concatenate(
        [shift_out(across[kx], 1 - ky, width) for ky in range(3) for kx in range(3)], 1
    )


def full_taps_back(grad, width):
    channels = grad.shape[1] // 9
    total = None
    for kx in range(3):
        column = None
        for ky in range(3):
            t = 3 * ky + kx
            v = shift_out(grad[:, t * channels : (t + 1) * channels], ky - 1, width)
            column = v if column is None else column + v
        column = shift_in(column, kx - 1, width)
        total = column if total is None else total + column
    return total


HY = 16
HX = 32
CELLS = HY * HX


def region_kernel(
    slab_ref, counts_ref, bird_ref, anchors_ref, goals_ref, shards_ref,
    maps_ref, grad_ref, quarter_ref,
    wv, edge, gr, sems,
    l1_scr, l2_scr, z1_scr, zu1_scr, zu2_scr, zu3_scr, head_scr, maps_scr, two_scr, three_scr, plane_scr,
):
    slab = slab_ref[0]

    def local(tile, s):
        return PAD_T * s + tile - (STRIDE_T * s - 1)

    copies = []
    ends = [PLANE_T0] + [STRIDE_T * s - 1 for s in range(1, SLABS)] + [PLANE_T0 + PLANE_T]
    for s in range(SLABS):
        low = ends[s] + (2 if s > 0 else 0)
        size = ends[s + 1] - low
        copies.append(
            pltpu.make_async_copy(
                shards_ref.at[pl.ds(local(low, s), size)],
                wv.at[pl.ds(low - PLANE_T0, size)],
                sems.at[len(copies)],
            )
        )
    for s in range(1, SLABS):
        for k in range(2):
            copies.append(
                pltpu.make_async_copy(
                    shards_ref.at[pl.ds(local(ends[s], s - 1 + k), 2)],
                    edge.at[pl.ds(4 * (s - 1) + 2 * k, 2)],
                    sems.at[len(copies)],
                )
            )
    for c in copies:
        c.start()
    gr[0 : PLANE_T0 + 1] = jnp.zeros((PLANE_T0 + 1, TILE, LANES), f32)
    gr[PLANE_T0 + 1 + PLANE_T : GRAD_T] = jnp.zeros((GRAD_T - PLANE_T0 - 1 - PLANE_T, TILE, LANES), f32)
    for c in copies:
        c.wait()
    for s in range(1, SLABS):
        at = ends[s] - PLANE_T0
        wv[at : at + 2] = edge[4 * (s - 1) : 4 * s - 2] + edge[4 * s - 2 : 4 * s]

    def narrow(tile, rows):
        at = tile - PLANE_T0
        return wv[at : at + rows // 16].reshape(rows, LANES)

    def wide(tile, rows):
        at = tile - PLANE_T0
        both = wv[at : at + rows // 8].reshape(rows // 16, 2, TILE, LANES)
        return jnp.concatenate(
            [both[:, 0].reshape(rows, LANES), both[:, 1].reshape(rows, LANES)], 1
        )

    def keep_narrow(tile, value):
        at = tile + 1
        tiles = value.shape[0] // 16
        gr[at : at + tiles] = value.reshape(tiles, TILE, LANES)

    def keep_wide(tile, value):
        at = tile + 1
        tiles = value.shape[0] // 16
        left = value[:, 0:128].reshape(tiles, 1, TILE, LANES)
        right = value[:, 128:256].reshape(tiles, 1, TILE, LANES)
        gr[at : at + 2 * tiles] = jnp.concatenate([left, right], 1).reshape(2 * tiles, TILE, LANES)

    t_one, t_two, t_three, t_up1, t_up2, t_up3, t_head = 225, 297, 369, 513, 657, 721, 1233

    bird = [
        jnp.concatenate([bird_ref[s, p] for s in range(SLABS)], 0).astype(f32) for p in range(4)
    ]
    taps_one = stride_taps(bird, 32)
    z1 = mm(taps_one, narrow(t_one, 1152))
    z1_scr[...] = z1
    level_one = silu(z1).astype(bf16).astype(f32)
    l1_scr[...] = level_one
    taps_two = stride_taps(split_planes(l1_scr, 16, 32), 16)
    z2 = mm(taps_two, narrow(t_two, 1152))
    level_two = silu(z2).astype(bf16)
    l2_scr[...] = level_two.astype(f32)
    taps_three = stride_taps(split_planes(l2_scr, 8, 16), 8)
    z3 = mm(taps_three, wide(t_three, 1152))
    level_three = silu(z3).astype(bf16)

    taps_up = full_taps(level_one, 32)
    zu1_scr[...] = mm(taps_up, wide(t_up1, 1152))
    for g in range(4):
        zu2_scr[g] = mm(level_two, wide(t_up2 + 16 * g, 128))
    for g in range(16):
        zu3_scr[g] = mm(level_three, wide(t_up3 + 32 * g, 256))

    lane = lane_of((96, LANES))
    rows = narrow(t_head, 96).astype(f32)
    for c in range(8):
        head_scr[pl.ds(c, 96, stride=8), :] = jnp.where(lane < 16, lane_roll(rows, -16 * c), 0.0)
    head = head_scr[...].astype(bf16)
    head_a, head_b, head_c = head[0:256], head[256:512], head[512:768]
    joined_a = silu(zu1_scr[...]).astype(bf16)
    for g in range(4):
        p, q = g // 2, g % 2
        part = mm(silu(zu2_scr[g]).astype(bf16), head_b)
        for a in range(8):
            two_scr[pl.ds((2 * a + p) * HX + q, 16, stride=2), :] = part[16 * a : 16 * a + 16]
    for g in range(16):
        p, q = g // 4, g % 4
        part = mm(silu(zu3_scr[g]).astype(bf16), head_c)
        for a in range(4):
            three_scr[pl.ds((4 * a + p) * HX + q, 8, stride=4), :] = part[8 * a : 8 * a + 8]
    maps = mm(joined_a, head_a) + two_scr[...] + three_scr[...]
    maps = jnp.transpose(maps)[0:16]
    own = jnp.zeros((16, 128), f32)
    for s in range(SLABS):
        own = own + jnp.where(slab == s, maps[:, 128 * s : 128 * s + 128], 0.0)
    maps_ref[...] = own

    live_count = counts_ref[0]
    anchors = anchors_ref[...]
    slot = row_of((40, CELLS))
    place = lane_of((40, CELLS))
    positive = [
        jnp.sum(
            jnp.logical_and(anchors == place + k * CELLS, slot < live_count).astype(f32),
            axis=0,
            keepdims=True,
        )
        for k in range(2)
    ]
    row = row_of((16, CELLS))
    second = jnp.logical_or(row == 1, row >= 9)
    marked = jnp.where(second, positive[1], positive[0])
    share = 1.0 / jnp.maximum(live_count.astype(f32), 1.0)
    class_grad = (sigmoid(maps) - marked) * (1.0 / (2.0 * CELLS))
    box_grad = jnp.clip(maps - goals_ref[...], -1.0, 1.0) * marked * share
    dmaps = jnp.where(row < 2, class_grad, box_grad)
    dmaps = jnp.transpose(jnp.concatenate([dmaps, jnp.zeros((LANES - 16, CELLS), f32)], 0))
    maps_scr[...] = dmaps
    low = dmaps.astype(bf16)

    dhead_a = mm_tn(joined_a, low)
    dz = mm_nt(low, head_a) * silu_slope(zu1_scr[...])
    dz = dz.astype(bf16)
    keep_wide(t_up1, mm_tn(taps_up, dz))
    dlevel_one = full_taps_back(mm_nt(dz, wide(t_up1, 1152)), 32)

    dhead_b = jnp.zeros((256, LANES), f32)
    dlevel_two = jnp.zeros((128, 128), f32)
    for g in range(4):
        p, q = g // 2, g % 2
        part = jnp.concatenate(
            [maps_scr[pl.ds((2 * a + p) * HX + q, 16, stride=2), :] for a in range(8)], 0
        ).astype(bf16)
        z = zu2_scr[g]
        dhead_b = dhead_b + mm_tn(silu(z).astype(bf16), part)
        dz = (mm_nt(part, head_b) * silu_slope(z)).astype(bf16)
        keep_wide(t_up2 + 16 * g, mm_tn(level_two, dz))
        dlevel_two = dlevel_two + mm_nt(dz, wide(t_up2 + 16 * g, 128))
    dhead_c = jnp.zeros((256, LANES), f32)
    dlevel_three = jnp.zeros((32, 256), f32)
    for g in range(16):
        p, q = g // 4, g % 4
        part = jnp.concatenate(
            [maps_scr[pl.ds((4 * a + p) * HX + q, 8, stride=4), :] for a in range(4)], 0
        ).astype(bf16)
        z = zu3_scr[g]
        dhead_c = dhead_c + mm_tn(silu(z).astype(bf16), part)
        dz = (mm_nt(part, head_c) * silu_slope(z)).astype(bf16)
        keep_wide(t_up3 + 32 * g, mm_tn(level_three, dz))
        dlevel_three = dlevel_three + mm_nt(dz, wide(t_up3 + 32 * g, 256))

    head_scr[...] = jnp.concatenate([dhead_a, dhead_b, dhead_c], 0)
    rows = jnp.zeros((96, LANES), f32)
    for c in range(8):
        piece = jnp.where(lane < 16, head_scr[pl.ds(c, 96, stride=8), :], 0.0)
        rows = rows + lane_roll(piece, 16 * c)
    keep_narrow(t_head, rows)

    dz = (dlevel_three * silu_slope(z3)).astype(bf16)
    keep_wide(t_three, mm_tn(taps_three, dz))
    merge_planes(l2_scr, stride_taps_back(mm_nt(dz, wide(t_three, 1152)), 8), 8, 16)
    dlevel_two = dlevel_two + l2_scr[...]
    dz = (dlevel_two * silu_slope(z2)).astype(bf16)
    keep_narrow(t_two, mm_tn(taps_two, dz))
    merge_planes(l1_scr, stride_taps_back(mm_nt(dz, narrow(t_two, 1152)), 16), 16, 32)
    dlevel_one = dlevel_one + l1_scr[...]
    dz = (dlevel_one * silu_slope(z1_scr[...])).astype(bf16)
    keep_narrow(t_one, mm_tn(taps_one, dz))
    planes = stride_taps_back(mm_nt(dz, narrow(t_one, 1152)), 32)
    for p in range(4):
        plane_scr[p] = planes[p]
    at = pl.multiple_of(slab * 128, 128)
    for p in range(4):
        grad_ref[p] = plane_scr[p, pl.ds(at, 128), :].astype(bf16)
    out = pltpu.make_async_copy(gr.at[pl.ds(STRIDE_T * slab, SHARD_T)], quarter_ref, sems.at[0])
    out.start()
    out.wait()


def region(slab, counts, bird, anchors, goals, shards):
    return call(
        region_kernel,
        (
            shape((16, 128)),
            shape((4, 128, LANES), bf16),
            shape((SHARD_T, TILE, LANES)),
        ),
        [smem(), smem(), vmem(), vmem(), vmem(), anywhere()],
        (vmem(), vmem(), anywhere()),
        [
            pltpu.VMEM((PLANE_T, TILE, LANES), bf16),
            pltpu.VMEM((12, TILE, LANES), bf16),
            pltpu.VMEM((GRAD_T, TILE, LANES), f32),
            pltpu.SemaphoreType.DMA((10,)),
            pltpu.VMEM((512, 128), f32),
            pltpu.VMEM((128, 128), f32),
            pltpu.VMEM((512, 128), f32),
            pltpu.VMEM((512, 256), f32),
            pltpu.VMEM((4, 128, 256), f32),
            pltpu.VMEM((16, 32, 256), f32),
            pltpu.VMEM((768, LANES), f32),
            pltpu.VMEM((512, LANES), f32),
            pltpu.VMEM((512, LANES), f32),
            pltpu.VMEM((512, LANES), f32),
            pltpu.VMEM((4, 512, LANES), f32),
        ],
    )(slab, counts, bird, anchors, goals, shards)


def body(
    points, point_counts, voxel_cells, pos_anchors, pos_counts, reg_targets, params, moment1, moment2
):
    everyone = ("batch", "slab")
    batches = lax.axis_size("batch")
    devices = batches * SLABS
    slab = lax.axis_index("slab")
    slab_arg = slab.astype(jnp.int32).reshape(1)
    flat_rows = jnp.pad(params, (0, FLAT_R * LANES - SHARD)).reshape(FLAT_R, LANES)
    own = spread_shard(slab_arg, flat_rows)

    small = lax.all_gather(own[0:10], "slab", axis=0, tiled=True)[0:10]
    share = PAD_T // batches
    chunk = lax.dynamic_slice_in_dim(own, lax.axis_index("batch") * share, share, 0)
    shards = lax.all_gather(chunk, ("slab", "batch"), axis=0, tiled=True)
    conv_rows = shards[10 : 10 + CONV_R // TILE].reshape(CONV_R, LANES)

    counts = point_counts.reshape(1, VOX)
    features = encode(points, counts, voxel_cells.reshape(1, VOX), small)
    features = lax.all_gather(features, "slab", axis=0)
    bird, *kept = volume(slab_arg, features, conv_rows)
    birds = lax.all_gather(bird, "slab", axis=0)
    goals = jnp.pad(reg_targets.reshape(14, CELLS), ((2, 0), (0, 0)))
    maps, bird_grad, quarter = region(
        slab_arg, pos_counts, birds, pos_anchors.reshape(40, 1), goals, shards
    )
    quarter = lax.psum(quarter, "batch")
    feature_grad, conv_grad = volume_back(slab_arg, features, bird_grad, kept)
    feature_grad = lax.all_to_all(feature_grad, "slab", 0, 0, tiled=True)
    points_grad, vfe_grad = encode_back(points, counts, small, feature_grad)

    early = jnp.concatenate([vfe_grad, conv_grad], 0).astype(bf16)
    early = jnp.pad(early, ((0, CONV_T * TILE - early.shape[0]), (0, 0)))
    early = early.reshape(devices, CONV_T * TILE // devices, LANES)
    early = lax.all_to_all(early, everyone, 0, 0, tiled=True)
    early = jnp.sum(early.astype(f32), axis=0).astype(bf16)
    early = lax.all_gather(early, everyone, axis=0, tiled=True)
    grads, squares = gather_shard(slab_arg, quarter, early)
    grad_norm = jnp.sqrt(lax.psum(jnp.sum(squares), "slab"))
    own_grads = grads.reshape(-1)[0:SHARD]
    clipped = own_grads * (clip_level / jnp.maximum(grad_norm, clip_level))
    new_moment1 = beta_one * moment1 + (1.0 - beta_one) * clipped
    new_moment2 = beta_two * moment2 + (1.0 - beta_two) * clipped * clipped
    direction = (
        new_moment1
        / (1.0 - beta_one**STEP)
        / (jnp.sqrt(new_moment2 / (1.0 - beta_two**STEP)) + adam_eps)
    )
    new_params = params - learn_rate * (direction + weight_decay * params)
    head_maps = maps.reshape(1, 16, HY // SLABS, HX)
    return (head_maps, points_grad, new_moment1, new_moment2, new_params, grad_norm)


def solution(mesh):
    in_specs = (
        P(None, None, ("batch", "slab")),
        P(("batch", "slab")),
        P(("batch", "slab")),
        P("batch", None),
        P("batch"),
        P("batch", None, None, None),
        P("slab"),
        P("slab"),
        P("slab"),
    )
    out_specs = (
        P("batch", None, "slab", None),
        P(None, None, ("batch", "slab")),
        P("slab"),
        P("slab"),
        P("slab"),
        P(),
    )
    return jax.shard_map(body, mesh=mesh, in_specs=in_specs, out_specs=out_specs, check_vma=False)
```

time: 1050 us -> 366 us (0.35)
  waiting for transfers between devices: 430 us -> 161 us
  local copies, waits for them, and re-layouts: 273 us -> 11.5 us
  matrix products: 249 us -> 0 us
  Pallas kernels: 0 us -> 85.8 us
  blocking collectives: 0 us -> 65.9 us
  other arithmetic: 42.1 us -> 14.4 us
  starting transfers between devices: 26.1 us -> 6.98 us
    conv_general_dilated x21 -> x0, matrix products: 192 us -> none  [the longest x9 167 us: conv_volume(): lax.conv_general_dilated(volume, kernel, (stride, 1, 1), ((pad_depth, pad...]
    unnamed x4 -> x3, waiting for transfers between devices: 185 us -> 0.73 us
    psum x1, waiting for transfers between devices: 200 us -> 46.4 us  [body(): quarter = lax.psum(quarter, 'batch')]
    concatenate x1 -> x0, local copies, waits for them, and re-layouts: 91.9 us -> none  [body(): flat_grad = jnp.concatenate([piece.reshape(-1) for piece in local_grads])]
    pallas_call x0 -> x7, Pallas kernels: none -> 85.8 us  [the longest x1 23.2 us: volume_back(): call(volume_back_kernel, (shape((SLABS, FC, VOX), bf16), shape((CONV_R, L...]
    all_gather x1 -> x2, waiting for transfers between devices: 20.7 us -> 78.4 us  [the longest x1 57.3 us: body(): early = lax.all_gather(early, everyone, axis=0, tiled=True)]
    dot_general x18 -> x0, matrix products: 57.1 us -> none  [the longest x3 30.5 us: vfe_forward(): jnp.einsum('oc,cpv->opv', vfe_three, joined_two, precision=highest)]
    all_gather x0 -> x3, blocking collectives: none -> 54.1 us  [the longest x1 21.7 us: body(): features = lax.all_gather(features, 'slab', axis=0)]
  transfers between devices with their start and end apart: 13 -> 5, of which waited for: 8 -> 5; matrix products, arithmetic and copies ran while one was open for 14% -> 2% of each run, Pallas kernels for 0% -> 3%
where the time goes in v1:
time: 366 us; the launch traced here: 363 us
  waiting for transfers between devices  161 us (44%)
  Pallas kernels  85.8 us (23%)
  blocking collectives  65.9 us (18%)
  between operations  16.5 us (5%)
  other arithmetic  14.4 us (4%)
  local copies, waits for them, and re-layouts  11.5 us (3%)
  starting transfers between devices  6.98 us (2%)
    all_gather x1, waiting for transfers between devices, body(): early = lax.all_gather(early, everyone, axis=0, tiled=True)  57.3 us
    psum x1, waiting for transfers between devices, body(): quarter = lax.psum(quarter, 'batch')  46.4 us
    all_to_all x1, waiting for transfers between devices, body(): early = lax.all_to_all(early, everyone, 0, 0, tiled=True)  24.2 us
    pallas_call x1, Pallas kernels, volume_back(): call(volume_back_kernel, (shape((SLABS, FC, VOX), bf16), shape((CONV_R, L...  23.2 us
    all_gather x1, blocking collectives, body(): features = lax.all_gather(features, 'slab', axis=0)  21.7 us
    all_gather x1, waiting for transfers between devices, body(): shards = lax.all_gather(chunk, ('slab', 'batch'), axis=0, tiled=True)  21.1 us
    pallas_call x1, Pallas kernels, encode_back(): call(encode_back_kernel, (shape((7, PTS, VOX)), shape((160, LANES))), [vm...  20.3 us
    all_gather x1, blocking collectives, body(): birds = lax.all_gather(bird, 'slab', axis=0)  17.1 us
  transfers between devices with their start and end apart: 5, of which 5 were waited for; matrix products, arithmetic and copies ran while one was open for 2% of the time, Pallas kernels for 3%

profile of v1, /device:TPU:0, one launch (start us, length us, event | category | flops | bytes accessed | tf_op | source)
XLA Modules:
  0.0 362.6 jit_solution(12077284720678041478)
XLA Ops:
  7.2 0.0 all-gather.5.cloned.1.call-start
  7.2 3.3 pad_bitcast_fusion.flat_ref
  10.6 0.0 copy-start.4
  10.6 0.0 copy-start.2
  10.6 4.2 %shard_map.136 = bf16[320,16,128]{2,1,0:T(8,128)(2,1)} custom-call(s32[1]{0:T(128)} %bitcast.slab_ref, f32[4960,128]{1,0:T(8,128)} %pad_bitcast_fusion.flat_ref), custom_call_target="tpu_custom_call" | custom-call | tf_op jit(solution)/shard_map/pallas_call | solution.py:175
  14.7 1.6 constant_dynamic-slice_fusion
  16.3 0.0 all-gather.5.cloned.1.call-update
  16.4 0.8 slice.16
  17.8 0.0 copy-done.4
  17.8 0.7 copy.16.anchors_ref
  18.5 0.0 copy-done.2
  18.5 0.1 reshape.48
  18.6 15.3 %all_gather.21 = bf16[40,16,128]{2,1,0:T(8,128)(2,1)S(1)} all-gather(bf16[10,16,128]{2,1,0:T(8,128)(2,1)S(1)} %slice.16), channel_id=1, replica_groups=mesh['batch'=8,'slab'=4] {'slab'}, dimensions={0}, use_global_device_ids=true | all-gather | bytes 204800 | tf_op jit(solution)/shard_map/all_gather | solution.py:1062
  33.9 0.6 slice.17.rows_ref
  34.5 0.6 pad.13.goals_ref
  35.1 9.8 %shard_map.137 = bf16[144,512]{1,0:T(8,128)(2,1)} custom-call(bf16[7,35,512]{2,1,0:T(8,128)(2,1)} %points_ref.3, s32[1,512]{1,0:T(1,128)} %bitcast.18, s32[1,512]{1,0:T(1,128)} %bitcast.20, bf16[10,16,128]{2,1,0:T(8,128)(2,1)} %slice.17.rows_ref), custom_call_target="tpu_custom_call" | custom-call | tf_op jit(solution)/shard_map/pallas_call | solution.py:374
  44.9 21.7 %all-gather = bf16[576,512]{1,0:T(8,128)(2,1)} all-gather(bf16[144,512]{1,0:T(8,128)(2,1)} %shard_map.137), channel_id=2, replica_groups=mesh['batch'=8,'slab'=4] {'slab'}, dimensions={0}, use_global_device_ids=true | all-gather | bytes 737280 | tf_op jit(solution)/shard_map/all_gather | solution.py:1070
  66.7 21.1 %all-gather.5.cloned.1.call-done.shards_ref = bf16[1280,16,128]{2,1,0:T(8,128)(2,1)} async-done(((bf16[40,16,128]{2,1,0:T(8,128)(2,1)}), bf16[1280,16,128]{2,1,0:T(8,128)(2,1)}) %all-gather.5.cloned.1.call-update) | async-done | bytes 5242896 | tf_op jit(solution)/shard_map/all_gather | solution.py:1065
  87.8 2.2 slice.18
  90.0 10.6 %shard_map.138 = (bf16[4,128,128]{2,1,0:T(8,128)(2,1)}, bf16[9,896,128]{2,1,0:T(8,128)(2,1)}, bf16[6,768,128]{2,1,0:T(8,128)(2,1)}, bf16[6,640,128]{2,1,0:T(8,12...) custom-call(s32[1]{0:T(128)} %bitcast.slab_ref, ...), custom_call_target="tpu_custom_call" | custom-call | tf_op jit(solution)/shard_map/pallas_call | solution.py:646
  100.6 17.1 %all-gather.1 = bf16[16,128,128]{2,1,0:T(8,128)(2,1)} all-gather(bf16[4,128,128]{2,1,0:T(8,128)(2,1)} %get-tuple-element.25), channel_id=3, replica_groups=mesh['batch'=8,'slab'=4] {'slab'}, dimensions={0}, use_global_device_ids=true | all-gather | bytes 655360 | tf_op jit(solution)/shard_map/all_gather | solution.py:1072
  117.7 13.1 %shard_map.139 = (f32[16,128]{1,0:T(8,128)}, bf16[4,128,128]{2,1,0:T(8,128)(2,1)}, f32[312,16,128]{2,1,0:T(8,128)}) custom-call(s32[1]{0:T(128)} %bitcast.slab_ref, s32[1]{0:T(128)S(6)} %copy.18.counts_ref, bf16[4,4,128,128]{3,2,1,0:T(8,128)(2,1)} %bitcast.17, s32[40,1]{1,0:T(8,128)} %copy.16.anchors_ref, f32[16,512]{1,0:T(8,128)} %pad.13.goals_ref, ...), custom_call_target="tpu_custom_call" | custom-call | tf_op jit(solution)/shard_map/pallas_call | solution.py:1022
  130.8 23.2 %shard_map.140 = (bf16[4,128,512]{2,1,0:T(8,128)(2,1)}, f32[3456,128]{1,0:T(8,128)}) custom-call(s32[1]{0:T(128)} %bitcast.slab_ref, bf16[4,144,512]{2,1,0:T(8,128)(2,1)} %bitcast.14, bf16[4,128,128]{2,1,0:T(8,128)(2,1)} %get-tuple-element.27.bird_ref, bf16[9,896,128]{2,1,0:T(8,128)(2,1)} %get-tuple-element.28.grid_ref, ...), custom_call_target="tpu_custom_call" | custom-call | tf_op jit(solution)/shard_map/pallas_call | solution.py:733
  154.0 3.5 all-to-all-start
  157.5 1.6 convert.8
  159.1 11.8 %all-to-all-done.grad_ref = bf16[4,128,512]{2,1,0:T(8,128)(2,1)S(1)} async-done(((bf16[4,128,512]{2,1,0:T(8,128)(2,1)}), bf16[4,128,512]{2,1,0:T(8,128)(2,1)S(1)}, u32[]{:S(2)}, u32[]{:S(2)}) %all-to-all-start) | async-done | bytes 524320 | tf_op jit(solution)/shard_map/all_to_all | solution.py:1079
  170.8 0.8 copy-done.1
  171.6 20.3 %shard_map.141 = (f32[7,35,512]{2,1,0:T(8,128)}, f32[160,128]{1,0:T(8,128)}) custom-call(bf16[7,35,512]{2,1,0:T(8,128)(2,1)} %points_ref.3, s32[1,512]{1,0:T(1,128)} %bitcast.19, bf16[10,16,128]{2,1,0:T(8,128)(2,1)} %slice.17.rows_ref, bf16[4,128,512]{2,1,0:T(8,128)(2,1)} %copy-done.1), custom_call_target="tpu_custom_call" | custom-call | tf_op jit(solution)/shard_map/pallas_call | solution.py:465
  191.9 0.9 convert.7
  192.8 1.0 fusion.3
  193.8 3.4 all-to-all-start.1
  197.2 0.0 all-reduce.5.cloned.1.call-start
  197.3 0.7 all-reduce.5.cloned.1.call-update
  198.0 0.0 copy-start.3
  198.0 0.0 copy-start
  198.0 0.0 all-gather.7.cloned.1.call-start
  198.0 24.2 %all-to-all-done.1 = bf16[32,128,128]{2,1,0:T(8,128)(2,1)} async-done(((bf16[32,128,128]{2,1,0:T(8,128)(2,1)}), bf16[32,128,128]{2,1,0:T(8,128)(2,1)}, u32[]{:S(2)}, u32[]{:S(2)}) %all-to-all-start.1) | async-done | bytes 1048608 | tf_op jit(solution)/shard_map/all_to_all | solution.py:1085
  222.2 2.0 reduce_sum.21
  224.2 0.0 all-gather.7.cloned.1.call-update
  224.3 46.4 %all-reduce.5.cloned.1.call-done.quarter_ref = f32[312,16,128]{2,1,0:T(8,128)} async-done(((f32[312,16,128]{2,1,0:T(8,128)}), f32[312,16,128]{2,1,0:T(8,128)}) %all-reduce.5.cloned.1.call-update) | async-done | bytes 2555920 | tf_op jit(solution)/shard_map/psum | solution.py:1077
  270.6 57.3 %all-gather.7.cloned.1.call-done.early_ref = bf16[4096,128]{1,0:T(8,128)(2,1)} async-done(((bf16[128,128]{1,0:T(8,128)(2,1)}), bf16[4096,128]{1,0:T(8,128)(2,1)}) %all-gather.7.cloned.1.call-update) | async-done | bytes 1048592 | tf_op jit(solution)/shard_map/all_gather | solution.py:1087
  327.9 4.7 %shard_map.142 = (f32[4960,128]{1,0:T(8,128)}, f32[8,128]{1,0:T(8,128)}) custom-call(s32[1]{0:T(128)} %bitcast.slab_ref, f32[312,16,128]{2,1,0:T(8,128)} %all-reduce.5.cloned.1.call-done.quarter_ref, bf16[4096,128]{1,0:T(8,128)(2,1)} %all-gather.7.cloned.1.call-done.early_ref), custom_call_target="tpu_custom_call" | custom-call | tf_op jit(solution)/shard_map/pallas_call | solution.py:229
  332.6 1.3 reduce_sum.22
  333.9 0.0 copy-done.3
  333.9 0.7 reshape.49
  334.6 11.7 %psum.15 = f32[]{:T(128)} all-reduce(f32[]{:T(128)} %reduce_sum.22), channel_id=1, replica_groups=mesh['batch'=8,'slab'=4] {'slab'}, use_global_device_ids=true, to_apply=%region_3.4 | all-reduce | flops 1 | bytes 8 | tf_op jit(solution)/shard_map/psum | solution.py:1089
  347.1 0.0 copy-done
  347.1 7.6 %multiply_subtract_fusion = (f32[634396]{0:T(1024)}, f32[634396]{0:T(1024)}, f32[634396]{0:T(1024)}) fusion(f32[634396]{0:T(1024)S(1)} %copy-done, f32[]{:T(128)S(6)} %div.18, f32[634880]{0:T(1024)} %bitcast.16, f32[634396]{0:T(1024)} %param.17, f32[634396]{0:T(1024)} %param.16), kind=kLoop, calls=%fused_computation.3 | loop fusion | flops 10150336 | bytes 17763092 | tf_op jit(solution)/shard_map/sub | solution.py:1099
  (1 shorter events, 0.0 us)
Async XLA Ops:
  7.2 80.6 %all-gather.5.cloned.1.call-start = ((), (), s32[]{:S(2)}) async-start(), calls=%async_computation.2 | async-start | bytes 5406720 | tf_op jit(solution)/shard_map/all_gather | solution.py:1065
  10.6 7.2 %copy-start.4 = (s32[1,40]{1,0:T(1,128)S(1)}, s32[1,40]{1,0:T(1,128)}, u32[]{:S(2)}) copy-start(s32[1,40]{1,0:T(1,128)} %param.12) | copy-start | bytes 484
  10.6 7.9 %copy-start.2 = (f32[1,14,16,32]{3,2,1,0:T(8,128)S(1)}, f32[1,14,16,32]{3,2,1,0:T(8,128)}, u32[]{:S(2)}) copy-start(f32[1,14,16,32]{3,2,1,0:T(8,128)} %param.14) | copy-start | bytes 86020
  154.0 16.8 %all-to-all-start = ((bf16[4,128,512]{2,1,0:T(8,128)(2,1)}), bf16[4,128,512]{2,1,0:T(8,128)(2,1)S(1)}, u32[]{:S(2)}, u32[]{:S(2)}) async-start(bf16[4,128,512]{2,1,0:T(8,128)(2,1)} %get-tuple-element.37), calls=%async_computation | async-start | bytes 1048576 | tf_op jit(solution)/shard_map/all_to_all | solution.py:1079
  170.8 0.8 copy-start.1
  193.8 28.4 %all-to-all-start.1 = ((bf16[32,128,128]{2,1,0:T(8,128)(2,1)}), bf16[32,128,128]{2,1,0:T(8,128)(2,1)}, u32[]{:S(2)}, u32[]{:S(2)}) async-start(bf16[32,128,128]{2,1,0:T(8,128)(2,1)} %bitcast.8), calls=%async_computation.1 | async-start | bytes 2097152 | tf_op jit(solution)/shard_map/all_to_all | solution.py:1085
  197.2 73.4 %all-reduce.5.cloned.1.call-start = ((), (), s32[]{:S(2)}) async-start(), calls=%async_computation.3 | async-start | bytes 5111808 | tf_op jit(solution)/shard_map/psum | solution.py:1077
  198.0 135.9 %copy-start.3 = (f32[16,128]{1,0:T(8,128)S(1)}, f32[16,128]{1,0:T(8,128)}, u32[]{:S(2)}) copy-start(f32[16,128]{1,0:T(8,128)} %get-tuple-element.26) | copy-start | bytes 24580
  198.0 149.1 %copy-start = (f32[634396]{0:T(1024)S(1)}, f32[634396]{0:T(1024)}, u32[]{:S(2)}) copy-start(f32[634396]{0:T(1024)} %param.15) | copy-start | bytes 7612756
  198.0 129.9 %all-gather.7.cloned.1.call-start = ((), (), s32[]{:S(2)}) async-start(), calls=%async_computation.4 | async-start | bytes 1081344 | tf_op jit(solution)/shard_map/all_gather | solution.py:1087
Sparse Core Ops, SparseCore 0:
  16.5 71.2 all-gather.4
  201.4 69.2 all-reduce.4
  274.6 53.2 all-gather.6
